TPU v7x, 256 devices: a whole 4x4x8 slice. The times are simulated.
256 devices in a mesh: dp: 16 (over z, core), seq: 16 (over x, y).
Axes of the slice: x: 4, y: 4, z: 8, core: 2. Of those that a mesh axis runs over, the one named last changes fastest.
Arguments:
- gated_part: bfloat16 [16, 3072, 4096], P('dp', 'seq'), may hold values from -6 to 6
- mixed_part: bfloat16 [16, 3072, 4096], P('dp', 'seq'), may hold values from -400 to 400
- out_grad: bfloat16 [16, 3072, 4096], P('dp', 'seq'), may hold values from -6 to 6
- norm_gain: float32 [4096], replicated, may hold values from 0.1 to 1.9
- mix_bias: float32 [3072], replicated, may hold values from -4 to 4
- token_mixing_weight: bfloat16 [18, 128, 128], replicated, may hold values from -0.125 to 0.125
- stride_cols: int32 [24, 2], replicated, may hold values from -1 to 7, as said below
Outputs:
- gated_grad: bfloat16 [16, 3072, 4096], P('dp', 'seq')
- value_grad: bfloat16 [16, 3072, 4096], P('dp', 'seq')
- weight_grad: float32 [18, 128, 128], replicated
- gain_grad: float32 [4096], replicated
- bias_grad: float32 [3072], P('seq')
Inputs may be any that keep to these rules, and one draw needn't show every extreme that they name: stride_cols[i, s] is -1 for row blocks i < 16, and otherwise a column block from 0 to i - 16; -1 means no strided block; stride_cols[23, 0] is 7.
All inputs are finite; a program needn't handle non-finite values.
Results may differ from a plain program's by a relative error of at most 0.0085.
Values may be sent and summed in bfloat16 or wider, within the bound.
A program may use at most 128 MiB of HBM per device.

v0:
```python
import math

import jax
import jax.numpy as jnp
from jax import lax
from jax.sharding import PartitionSpec as P

MIXING_BLOCK = 128
BAND_BLOCKS = 16
NSTR = 2


EPS = 1e-05


def slot_mask(shape):
    slot_idx = lax.broadcasted_iota(jnp.int32, shape, 0)
    row_idx = lax.broadcasted_iota(jnp.int32, shape, 1)
    col_idx = lax.broadcasted_iota(jnp.int32, shape, 2)
    return (slot_idx > 0) | (row_idx >= col_idx)


def band_matrix(weights, backward):
    group = 2
    columns = group + BAND_BLOCKS - 1
    row_ids = jnp.arange(group, dtype=jnp.int32)[:, None]
    col_ids = jnp.arange(columns, dtype=jnp.int32)[None, :]
    if backward:
        offsets = col_ids - row_ids
    else:
        offsets = row_ids + BAND_BLOCKS - 1 - col_ids
    valid = (offsets >= 0) & (offsets < BAND_BLOCKS)
    clipped = jnp.clip(offsets, 0, BAND_BLOCKS - 1)
    tiles = jnp.take(weights[:BAND_BLOCKS], clipped.reshape(-1), axis=0)
    tiles = tiles.reshape(group, columns, MIXING_BLOCK, MIXING_BLOCK)
    if backward:
        tiles = jnp.swapaxes(tiles, 2, 3)
    tiles = jnp.where(valid[:, :, None, None], tiles, jnp.zeros((), tiles.dtype))
    return tiles.transpose(0, 2, 1, 3).reshape(group * MIXING_BLOCK, columns * MIXING_BLOCK)


def band_apply(matrix, padded, num_blocks, width):
    group = 2
    span_len = (group + BAND_BLOCKS - 1) * MIXING_BLOCK

    def one_group(group_id):
        piece = lax.dynamic_slice_in_dim(padded, group_id * group * MIXING_BLOCK, span_len, 0)
        return jnp.dot(matrix, piece, preferred_element_type=jnp.float32)

    result = lax.map(one_group, jnp.arange(num_blocks // group, dtype=jnp.int32))
    return result.reshape(num_blocks, MIXING_BLOCK, width)


def strided_blocks(blocks, stride_cols, strided):
    valid_rows = stride_cols[:, strided] >= 0
    safe_cols = jnp.maximum(stride_cols[:, strided], 0)
    picked = jnp.take(blocks, safe_cols, axis=0)
    return (
        jnp.where(valid_rows[:, None, None], picked, jnp.zeros((), picked.dtype)),
        valid_rows,
        safe_cols,
    )


def mix_forward(blocks, weights, stride_cols, mix_bias):
    num_blocks, _, width = blocks.shape
    tokens = blocks.reshape(num_blocks * MIXING_BLOCK, width)
    front = jnp.zeros(((BAND_BLOCKS - 1) * MIXING_BLOCK, width), blocks.dtype)
    padded = jnp.concatenate([front, tokens], axis=0)
    mixed_sum = band_apply(band_matrix(weights, False), padded, num_blocks, width)
    for strided in range(NSTR):
        picked, valid_rows, safe_cols = strided_blocks(blocks, stride_cols, strided)
        mixed_sum = mixed_sum + jnp.einsum(
            "ab,nbc->nac",
            weights[BAND_BLOCKS + strided],
            picked,
            preferred_element_type=jnp.float32,
        )
    mixed_sum = mixed_sum + mix_bias.reshape(num_blocks, MIXING_BLOCK, 1)
    return (mixed_sum.astype(jnp.bfloat16), padded)


def mix_backward(dblocks, blocks, padded, weights, stride_cols):
    num_blocks, _, width = blocks.shape
    total_len = num_blocks * MIXING_BLOCK
    dtokens = dblocks.reshape(total_len, width)
    tail = jnp.zeros(((BAND_BLOCKS - 1) * MIXING_BLOCK, width), dblocks.dtype)
    padded_back = jnp.concatenate([dtokens, tail], axis=0)
    dnorm = band_apply(band_matrix(weights, True), padded_back, num_blocks, width)
    band_grads = []
    for offset in range(BAND_BLOCKS):
        start = (BAND_BLOCKS - 1 - offset) * MIXING_BLOCK
        shifted = lax.slice_in_dim(padded, start, start + total_len, axis=0).reshape(
            num_blocks, MIXING_BLOCK, width
        )
        band_grads.append(
            jnp.einsum("nac,nbc->ab", dblocks, shifted, preferred_element_type=jnp.float32)
        )
    far_grads = []
    block_ids = jnp.arange(num_blocks, dtype=jnp.int32)
    for strided in range(NSTR):
        picked, valid_rows, safe_cols = strided_blocks(blocks, stride_cols, strided)
        far_grads.append(
            jnp.einsum("nac,nbc->ab", dblocks, picked, preferred_element_type=jnp.float32)
        )
        scatter_term = jnp.einsum(
            "ab,nac->nbc",
            weights[BAND_BLOCKS + strided],
            dblocks,
            preferred_element_type=jnp.float32,
        )
        scatter_term = jnp.where(
            valid_rows[:, None, None], scatter_term, jnp.zeros((), jnp.float32)
        )
        one_hot = (block_ids[:, None] == safe_cols[None, :]).astype(jnp.float32)
        dnorm = dnorm + jnp.einsum(
            "ji,ibc->jbc", one_hot, scatter_term, precision=lax.Precision.HIGHEST
        )
    slot_grad = jnp.stack(band_grads + far_grads)
    slot_grad = jnp.where(slot_mask(slot_grad.shape), slot_grad, jnp.zeros((), jnp.float32))
    return (dnorm.astype(jnp.bfloat16), slot_grad)


def shards(gated_part, mixed_part, out_grad, norm_gain, mix_bias, token_mixing_weight, stride_cols):
    seq_parts = lax.axis_size("seq")
    batch_size = lax.axis_size("dp")
    gated_rows = gated_part[0]
    value_rows = mixed_part[0]
    grad_rows = out_grad[0]
    tok_local, half_width = gated_rows.shape
    slice_width = half_width // seq_parts
    total_len = tok_local * seq_parts
    num_blocks = total_len // MIXING_BLOCK
    values = value_rows.astype(jnp.float32)
    row_mean = jnp.mean(values, axis=1, keepdims=True)
    centered = values - row_mean
    row_var = jnp.mean(centered * centered, axis=1, keepdims=True)
    inv_std = lax.rsqrt(row_var + EPS)
    norm_hat = centered * inv_std
    normed = (norm_hat * norm_gain).astype(jnp.bfloat16)
    weights = jnp.where(
        slot_mask(token_mixing_weight.shape),
        token_mixing_weight,
        jnp.zeros((), token_mixing_weight.dtype),
    )

    def to_panels(rows):
        return rows.reshape(tok_local, seq_parts, slice_width)

    def to_blocks(panel):
        return panel.reshape(num_blocks, MIXING_BLOCK, slice_width)

    def to_columns(blocks):
        return blocks.reshape(total_len, 1, slice_width)

    panel_norm, panel_gated, panel_grad = (
        lax.all_to_all(to_panels(normed), "seq", split_axis=1, concat_axis=0, tiled=True),
        lax.all_to_all(to_panels(gated_rows), "seq", split_axis=1, concat_axis=0, tiled=True),
        lax.all_to_all(to_panels(grad_rows), "seq", split_axis=1, concat_axis=0, tiled=True),
    )
    blocks = to_blocks(panel_norm)
    mixed16, padded = mix_forward(blocks, weights, stride_cols, mix_bias)
    grad_blocks = to_blocks(panel_grad).astype(jnp.float32)
    gated_grad_blocks = (grad_blocks * mixed16.astype(jnp.float32)).astype(jnp.bfloat16)
    dmix16 = (grad_blocks * to_blocks(panel_gated).astype(jnp.float32)).astype(jnp.bfloat16)
    bias_part = jnp.sum(dmix16.astype(jnp.float32), axis=2).reshape(total_len)
    dnorm16, slot_grad = mix_backward(dmix16, blocks, padded, weights, stride_cols)
    back_gated, back_norm = (
        lax.all_to_all(
            to_columns(gated_grad_blocks), "seq", split_axis=0, concat_axis=1, tiled=True
        ),
        lax.all_to_all(to_columns(dnorm16), "seq", split_axis=0, concat_axis=1, tiled=True),
    )
    gated_grad_rows = back_gated.reshape(tok_local, half_width)
    dnorm_rows = back_norm.reshape(tok_local, half_width)
    dnorm_f32 = dnorm_rows.astype(jnp.float32)
    hat_grad = dnorm_f32 * norm_gain
    value_grad = inv_std * (
        hat_grad
        - jnp.mean(hat_grad, axis=1, keepdims=True)
        - norm_hat * jnp.mean(hat_grad * norm_hat, axis=1, keepdims=True)
    )
    gain_part = jnp.sum(dnorm_f32 * norm_hat, axis=0)
    slot_sum, gain_sum, bias_full = lax.psum((slot_grad, gain_part, bias_part), ("dp", "seq"))
    bias_rows = lax.dynamic_slice_in_dim(bias_full, lax.axis_index("seq") * tok_local, tok_local)
    weight_grad = slot_sum / math.sqrt(batch_size * total_len * half_width)
    gain_grad = gain_sum / math.sqrt(batch_size * total_len)
    bias_grad = bias_rows / math.sqrt(batch_size * half_width)
    return (
        gated_grad_rows[None],
        value_grad.astype(jnp.bfloat16)[None],
        weight_grad,
        gain_grad,
        bias_grad,
    )


def solution(mesh):
    placed = (P("dp", "seq", None), P("dp", "seq", None), P("dp", "seq", None), P(), P(), P(), P())
    return jax.shard_map(
        shards,
        mesh=mesh,
        in_specs=placed,
        out_specs=(P("dp", "seq", None), P("dp", "seq", None), P(), P(), P("seq")),
        check_vma=False,
    )
```

profile of v0, /device:TPU:1, one launch (start us, length us, event | category | flops | bytes accessed | tf_op | source)
XLA Modules:
  0.0 700.6 jit_solution(6946990155267597122)
XLA Ops:
  11.7 5.0 fusion.13
  16.7 7.7 %all-to-all-start.1 = ((bf16[192,16,256]{2,0,1:T(8,128)(2,1)}), bf16[192,16,256]{2,0,1:T(8,128)(2,1)S(1)}, u32[]{:S(2)}, u32[]{:S(2)}) async-start(bf16[192,16,256]{2,0,1:T(8,128)(2,1)} %fusion.13), calls=%async_computation.1 | async-start | bytes 3145728 | tf_op jit(solution)/shard_map/all_to_all | solution.py:157
  31.3 13.7 %all-to-all-done.1 = bf16[192,16,256]{2,0,1:T(8,128)(2,1)S(1)} async-done(((bf16[192,16,256]{2,0,1:T(8,128)(2,1)}), bf16[192,16,256]{2,0,1:T(8,128)(2,1)S(1)}, u32[]{:S(2)}, u32[]{:S(2)}) %all-to-all-start.1) | async-done | bytes 1572896 | tf_op jit(solution)/shard_map/all_to_all | solution.py:157
  45.1 5.4 all-to-all-start
  62.2 8.1 %all-to-all-done = bf16[192,16,256]{2,0,1:T(8,128)(2,1)} async-done(((bf16[192,16,256]{2,0,1:T(8,128)(2,1)}), bf16[192,16,256]{2,0,1:T(8,128)(2,1)}, u32[]{:S(2)}, u32[]{:S(2)}) %all-to-all-start) | async-done | bytes 1572896 | tf_op jit(solution)/shard_map/all_to_all | solution.py:159
  70.3 5.0 all-to-all-start.3
  77.3 50.6 %while.24 = (s32[]{:T(128)}, f32[12,256,256]{2,1,0:T(8,128)}, s32[12]{0:T(128)S(1)}, bf16[4992,256]{1,0:T(8,128)(2,1)}, bf16[256,2176]{1,0:T(8,128)(2,1)}, /*index=5*/s32[]{:T(128)}, s32[1]{0:T(128)}, s32[]{:T(128)}, s32[]{:T(128)}) while((s32[]{:T(128)}, f32[12,256,256]{2,1,0:T(8,128)}, s32[12]{0:T(128)S(1)}, bf16[4992,256]{1,0:T(8,128)(2,1)}, ...), condition=%wide.region_3.5_spmd, body=%wide.region_2.4_spmd.sunk | while | flops 285212672 | bytes 3539111 | solution.py:50
  131.5 24.7 %pad_slice_fusion = (bf16[3072,256]{1,0:T(8,128)(2,1)}, bf16[3072,256]{1,0:T(8,128)(2,1)}, bf16[3072,256]{1,0:T(8,128)(2,1)}, bf16[3072,256]{1,0:T(8,128)(2,1)},...) fusion(bf16[3072,256]{1,0:T(8,128)(2,1)S(1)} %bitcast.309), kind=kLoop, calls=%fused_computation.39 | loop fusion | bytes 25165824 | tf_op jit(solution)/shard_map/slice | solution.py:93
  172.9 3.9 reduce.6
  176.8 4.6 reshape.508
  181.4 7.0 %all-to-all-start.2 = ((bf16[16,2,24576]{2,1,0:T(2,128)(2,1)}), bf16[16,2,24576]{2,1,0:T(2,128)(2,1)}, u32[]{:S(2)}, u32[]{:S(2)}) async-start(bf16[16,2,24576]{2,1,0:T(2,128)(2,1)} %reshape.508), calls=%async_computation.2 | async-start | bytes 3145728 | tf_op jit(solution)/shard_map/all_to_all | solution.py:169
  188.4 3.6 copy.182
  197.0 46.5 %while.25 = (s32[]{:T(128)}, f32[12,256,256]{2,1,0:T(8,128)}, s32[12]{0:T(128)S(1)}, bf16[4992,256]{1,0:T(8,128)(2,1)}, bf16[256,2176]{1,0:T(8,128)(2,1)S(1)}, /...) while((s32[]{:T(128)}, f32[12,256,256]{2,1,0:T(8,128)}, s32[12]{0:T(128)S(1)}, ...), condition=%wide.region_5.8_spmd, body=%wide.region_4.7_spmd.sunk | while | flops 285212672 | bytes 3539111 | solution.py:50
  243.5 3.6 copy.185
  247.1 3.6 fusion.38
  257.1 4.9 reshape.510
  288.9 6.9 all-to-all-start.4
  299.7 266.1 %all-reduce.5.cloned.1.call-done = f32[18,128,128]{2,1,0:T(8,128)} async-done(((f32[18,128,128]{2,1,0:T(8,128)}), f32[18,128,128]{2,1,0:T(8,128)}) %all-reduce.5.cloned.1.call-update) | async-done | bytes 1179664 | tf_op jit(solution)/shard_map/psum | solution.py:184
  568.2 10.1 %reshape.509 = bf16[3072,1,256]{2,1,0:T(2,128)(2,1)} reshape(bf16[16,2,24576]{2,1,0:T(2,128)(2,1)} %all-to-all-done.2) | data formatting | bytes 3145728
  583.5 10.0 %reshape.511 = bf16[3072,1,256]{2,1,0:T(2,128)(2,1)} reshape(bf16[16,2,24576]{2,1,0:T(2,128)(2,1)} %all-to-all-done.4) | data formatting | bytes 3145728
  599.5 4.6 reshape.434
  604.1 5.1 multiply_reduce_fusion
  609.2 78.9 %all-reduce.2 = (f32[4096]{0:T(1024)S(1)}, f32[3072]{0:T(1024)S(1)}) all-reduce(f32[4096]{0:T(1024)S(1)} %bitcast.353, f32[3072]{0:T(1024)S(1)} %reshape.431), channel_id=1, replica_groups=mesh['dp'=16,'seq'=16] {'dp','seq'}, use_global_device_ids=true, to_apply=%region_10.13 | all-reduce | flops 7168 | bytes 57344 | tf_op jit(solution)/shard_map/psum | solution.py:184
  689.3 4.3 multiply_convert_fusion.1
  (260 shorter events, 183.0 us)
Async XLA Ops:
  7.2 1.9 copy-start.3
  9.0 2.1 copy-start.30
  16.7 8.0 %copy-start.29 = (bf16[18,128,128]{2,1,0:T(8,128)(2,1)S(1)}, bf16[18,128,128]{2,1,0:T(8,128)(2,1)}, u32[]{:S(2)}) copy-start(bf16[18,128,128]{2,1,0:T(8,128)(2,1)} %param.20) | copy-start | bytes 1769476
  16.7 28.3 %all-to-all-start.1 = ((bf16[192,16,256]{2,0,1:T(8,128)(2,1)}), bf16[192,16,256]{2,0,1:T(8,128)(2,1)S(1)}, u32[]{:S(2)}, u32[]{:S(2)}) async-start(bf16[192,16,256]{2,0,1:T(8,128)(2,1)} %fusion.13), calls=%async_computation.1 | async-start | bytes 3145728 | tf_op jit(solution)/shard_map/all_to_all | solution.py:157
  25.0 3.9 copy-start.27
  45.1 25.2 %all-to-all-start = ((bf16[192,16,256]{2,0,1:T(8,128)(2,1)}), bf16[192,16,256]{2,0,1:T(8,128)(2,1)}, u32[]{:S(2)}, u32[]{:S(2)}) async-start(bf16[192,16,256]{2,0,1:T(8,128)(2,1)} %copy.167), calls=%async_computation | async-start | bytes 3145728 | tf_op jit(solution)/shard_map/all_to_all | solution.py:159
  51.3 1.8 copy-start.28
  58.8 1.7 copy-start.32
  70.3 85.9 %all-to-all-start.3 = ((bf16[192,16,256]{2,0,1:T(8,128)(2,1)}), bf16[192,16,256]{2,0,1:T(8,128)(2,1)}, u32[]{:S(2)}, u32[]{:S(2)}) async-start(bf16[192,16,256]{2,0,1:T(8,128)(2,1)} %copy.176), calls=%async_computation.3 | async-start | bytes 3145728 | tf_op jit(solution)/shard_map/all_to_all | solution.py:158
  158.7 3.2 copy-start.2
  161.9 3.3 copy-start.23
  165.3 3.4 copy-start.31
  166.7 2.4 copy-start.7
  166.7 2.8 copy-start.25
  168.6 3.8 copy-start
  181.4 107.5 %all-to-all-start.2 = ((bf16[16,2,24576]{2,1,0:T(2,128)(2,1)}), bf16[16,2,24576]{2,1,0:T(2,128)(2,1)}, u32[]{:S(2)}, u32[]{:S(2)}) async-start(bf16[16,2,24576]{2,1,0:T(2,128)(2,1)} %reshape.508), calls=%async_computation.2 | async-start | bytes 3145728 | tf_op jit(solution)/shard_map/all_to_all | solution.py:169
  247.1 3.6 copy-start.5
  247.1 3.8 copy-start.6
  262.0 2.4 copy-start.1
  265.0 1.4 copy-start.22
  288.8 7.0 copy-start.26
  288.9 294.6 %all-to-all-start.4 = ((bf16[16,2,24576]{2,1,0:T(2,128)(2,1)}), bf16[16,2,24576]{2,1,0:T(2,128)(2,1)}, u32[]{:S(2)}, u32[]{:S(2)}) async-start(bf16[16,2,24576]{2,1,0:T(2,128)(2,1)} %reshape.510), calls=%async_computation.4 | async-start | bytes 3145728 | tf_op jit(solution)/shard_map/all_to_all | solution.py:172
  295.8 270.0 %all-reduce.5.cloned.1.call-start = ((), (), s32[]{:S(2)}) async-start(), calls=%async_computation.5 | async-start | bytes 2359296 | tf_op jit(solution)/shard_map/psum | solution.py:184
  604.1 85.2 %copy-start.4 = (bf16[1,192,4096]{2,1,0:T(8,128)(2,1)S(1)}, bf16[1,192,4096]{2,1,0:T(8,128)(2,1)}, u32[]{:S(2)}) copy-start(bf16[1,192,4096]{2,1,0:T(8,128)(2,1)} %param.16) | copy-start | bytes 4718596
  (15 other events, 21.1 us)
Sparse Core Ops, SparseCore 0:
  302.6 263.1 all-reduce.4
where the time goes:
time: 713 us; the launch traced here: 701 us
  waiting for transfers between devices  288 us (40%)
  local copies, waits for them, and re-layouts  145 us (20%)
  matrix products  85.8 us (12%)
  blocking collectives  78.9 us (11%)
  other arithmetic  40.2 us (6%)
  starting transfers between devices  32 us (4%)
  loops' own time  16.1 us (2%)
  between operations  14.7 us (2%)
    psum x1, waiting for transfers between devices, shards(): lax.psum((slot_grad, gain_part, bias_part), ('dp', 'seq'))  266 us
    psum x1, blocking collectives, shards(): lax.psum((slot_grad, gain_part, bias_part), ('dp', 'seq'))  78.9 us
    dot_general x24, matrix products, one_group(): return jnp.dot(matrix, piece, preferred_element_type=jnp.float32)  46.4 us
    unnamed x77, local copies, waits for them, and re-layouts  44.2 us
    slice x1, local copies, waits for them, and re-layouts, mix_backward(): lax.slice_in_dim(padded, start, start + total_len, axis=0)  24.7 us
    dynamic_update_slice x48, local copies, waits for them, and re-layouts, band_apply(): lax.map(one_group, jnp.arange(num_blocks // group, dtype=jnp.int32))  20.5 us
    dot_general x16, matrix products, mix_backward(): jnp.einsum('nac,nbc->ab', dblocks, shifted, preferred_element_type=jnp.fl...  19.2 us
    another operation x2, loops' own time, band_apply(): lax.map(one_group, jnp.arange(num_blocks // group, dtype=jnp.int32))  16.1 us
  transfers between devices with their start and end apart: 6, of which 3 were waited for; matrix products, arithmetic and copies ran while one was open for 29% of the time, Pallas kernels for 0%

commit v1 on v0

v1 whole, which is shorter than its diff:
```python
import math

import jax
import jax.numpy as jnp
from jax import lax
from jax.experimental import pallas as pl
from jax.experimental.pallas import tpu as pltpu
from jax.sharding import PartitionSpec as P

BLOCK = 128
BAND = 16
NSTR = 2
EPS = 1e-05
MESH = pl.DeviceIdType.MESH
F32 = jnp.float32
BF16 = jnp.bfloat16

OFFSETS = (
    (2, 2), (1, 2), (2, 1), (3, 2), (2, 3), (1, 1), (3, 3), (1, 3),
    (3, 1), (0, 2), (2, 0), (0, 1), (1, 0), (0, 3), (3, 0),
)

SEQ = 16
DP = 16
TOK = 192
FEAT = 4096
WIDTH = FEAT // SEQ
TOTAL = TOK * SEQ
GROUPS = TOTAL // (2 * BLOCK)
SPAN = (BAND + 1) * BLOCK
PAD = (BAND - 1) * BLOCK
SLOTS = BAND + NSTR
PIECE = SLOTS * BLOCK // DP
SUB = 16
REDUCERS = PIECE // SUB
CHUNK = 16

S_D, S_N, S_DN, S_MX, S_R1, S_R2, S_R2B, S_R3, S_BIAS, S_G1, S_G2 = range(11)
PHASES = 11
MIX_FIRST = 5


def rows(start, size):
    return pl.ds(pl.multiple_of(start, 16), size)


def lanes(start, size):
    return pl.ds(pl.multiple_of(start, 128), size)


def kernel(
    gated, value, grad, gain, bias, weights, cols,
    gated_grad, value_grad, weight_grad, gain_grad, bias_grad,
    u_ref, v_ref, g_ref, hat_ref, inv_ref,
    d_buf, n_buf, d_pad, n_pad, nt_pad, dn_all, mx_all, dn_back, mx_back,
    band, band_t, corner_t, wt_ref, picked, sums, slot_buf,
    r1, part, r2, r2b, r3_buf, r3, bias_acc, bias_all, g1_buf, g1, g2,
    in_sem, ss, rs,
):
    dp = lax.axis_index("dp")
    sq = lax.axis_index("seq")
    x, y = sq // 4, sq % 4

    def ahead(r):
        dx, dy = OFFSETS[r]
        return ((x + dx) % 4) * 4 + (y + dy) % 4

    def behind(r):
        dx, dy = OFFSETS[r]
        return ((x + 4 - dx) % 4) * 4 + (y + 4 - dy) % 4

    def to_seq(phase, r, src, dst):
        return pltpu.make_async_remote_copy(
            src_ref=src, dst_ref=dst, send_sem=ss.at[phase, r], recv_sem=rs.at[phase, r],
            device_id=(dp, ahead(r)), device_id_type=MESH,
        )

    def from_seq(phase, r, slot):
        pltpu.make_async_remote_copy(
            src_ref=slot, dst_ref=slot, send_sem=ss.at[phase, r], recv_sem=rs.at[phase, r],
            device_id=(dp, behind(r)), device_id_type=MESH,
        ).wait_recv()

    def to_dp(phase, r, src, dst):
        return pltpu.make_async_remote_copy(
            src_ref=src, dst_ref=dst, send_sem=ss.at[phase, r], recv_sem=rs.at[phase, r],
            device_id=((dp + r) % DP, sq), device_id_type=MESH,
        )

    def from_dp(phase, r, slot):
        pltpu.make_async_remote_copy(
            src_ref=slot, dst_ref=slot, send_sem=ss.at[phase, r], recv_sem=rs.at[phase, r],
            device_id=((dp + DP - r) % DP, sq), device_id_type=MESH,
        ).wait_recv()

    def other_dp(body):
        def step(r, carry):
            body(r)
            return carry

        lax.fori_loop(1, DP, step, 0)

    loads = [
        pltpu.make_async_copy(src, dst, in_sem.at[i])
        for i, (src, dst) in enumerate(((grad, g_ref), (gated, u_ref), (value, v_ref)))
    ]
    for load in loads:
        load.start()

    barrier = pltpu.get_barrier_semaphore()
    for r in range(SEQ - 1):
        pl.semaphore_signal(barrier, inc=1, device_id=(dp, ahead(r)), device_id_type=MESH)
    other_dp(
        lambda r: pl.semaphore_signal(
            barrier, inc=1, device_id=((dp + r) % DP, sq), device_id_type=MESH
        )
    )

    loads[0].wait()
    loads[1].wait()
    bias_acc[...] = jnp.zeros_like(bias_acc)

    def make_d(panel):
        at = lanes(panel * WIDTH, WIDTH)
        d = (g_ref[:, at].astype(F32) * u_ref[:, at].astype(F32)).astype(BF16)
        wide = d.astype(F32)
        bias_acc[...] += wide[:, :BLOCK] + wide[:, BLOCK:]
        return d

    my_rows = rows(sq * TOK, TOK)
    d_buf[ahead(0)] = make_d(ahead(0))
    pl.semaphore_wait(barrier, SEQ - 1 + DP - 1)
    for r in range(SEQ - 1):
        panel = ahead(r)
        if r > 0:
            d_buf[panel] = make_d(panel)
        to_seq(S_D, r, d_buf.at[panel], d_pad.at[my_rows]).start()
    d_pad[my_rows] = make_d(sq)

    loads[2].wait()

    def norm_rows(c, carry):
        at = rows(c * CHUNK, CHUNK)
        total = jnp.zeros((CHUNK, WIDTH), F32)
        for p in range(SEQ):
            total += v_ref[at, p * WIDTH : (p + 1) * WIDTH].astype(F32)
        mean = jnp.sum(total, axis=1, keepdims=True) * (1.0 / FEAT)
        total = jnp.zeros((CHUNK, WIDTH), F32)
        for p in range(SEQ):
            centered = v_ref[at, p * WIDTH : (p + 1) * WIDTH].astype(F32) - mean
            total += centered * centered
        inv = lax.rsqrt(jnp.sum(total, axis=1, keepdims=True) * (1.0 / FEAT) + EPS)
        inv_ref[at] = jnp.broadcast_to(inv, (CHUNK, BLOCK))
        for p in range(SEQ):
            cut = slice(p * WIDTH, (p + 1) * WIDTH)
            hat = (v_ref[at, cut].astype(F32) - mean) * inv
            hat_ref[at, cut] = hat
            n_buf[p, at] = (hat * gain[:, cut]).astype(BF16)
        return carry

    lax.fori_loop(0, TOK // CHUNK, norm_rows, 0)
    my_padded = rows(PAD + sq * TOK, TOK)
    for r in range(SEQ - 1):
        to_seq(S_N, r, n_buf.at[ahead(r)], n_pad.at[my_padded]).start()
    n_pad[my_padded] = n_buf[sq]

    part_bias = bias_acc[...].T.reshape(BLOCK // 8, 8, TOK)
    bias_all[dp] = jnp.sum(part_bias, axis=0)
    other_dp(lambda r: to_dp(S_BIAS, r, bias_all.at[dp], bias_all.at[dp]).start())

    zero_block = jnp.zeros((BLOCK, BLOCK), BF16)
    row_ids = lax.broadcasted_iota(jnp.int32, (BLOCK, BLOCK), 0)
    col_ids = lax.broadcasted_iota(jnp.int32, (BLOCK, BLOCK), 1)
    lower = row_ids >= col_ids
    for i, m in ((0, BAND), (1, 0)):
        for matrix in (band, band_t):
            matrix[i * BLOCK : (i + 1) * BLOCK, m * BLOCK : (m + 1) * BLOCK] = zero_block
    for k in range(SLOTS):
        w32 = weights[k].astype(F32)
        if k == 0:
            w32 = jnp.where(lower, w32, 0.0)
        w = w32.astype(BF16)
        wt32 = w32.T
        wt = wt32.astype(BF16)
        if k < BAND:
            for i in range(2):
                at = slice(i * BLOCK, (i + 1) * BLOCK)
                m = i + BAND - 1 - k
                band[at, m * BLOCK : (m + 1) * BLOCK] = w
                m = i + k
                band_t[at, m * BLOCK : (m + 1) * BLOCK] = wt
        else:
            wt_ref[k - BAND] = wt32

    far_rows = GROUPS * 2 - BAND

    def corner_row(j, carry):
        for i in range(far_rows):
            block = jnp.zeros((BLOCK, BLOCK), F32)
            for s in range(NSTR):
                hit = jnp.broadcast_to(cols[BAND + i : BAND + i + 1, s : s + 1], (BLOCK, BLOCK)) == j
                block += jnp.where(hit, wt_ref[s], 0.0)
            corner_t[rows(j * BLOCK, BLOCK), i * BLOCK : (i + 1) * BLOCK] = block.astype(BF16)
        return carry

    lax.fori_loop(0, far_rows, corner_row, 0)
    d_pad[TOTAL:] = jnp.zeros((PAD, WIDTH), BF16)
    n_pad[:PAD] = jnp.zeros((PAD, WIDTH), BF16)
    nt_pad[:, :PAD] = jnp.zeros((WIDTH, PAD), BF16)
    nt_pad[:, PAD + TOTAL :] = jnp.zeros((WIDTH, BLOCK), BF16)

    for r in range(SEQ - 1):
        from_seq(S_D, r, d_pad.at[rows(behind(r) * TOK, TOK)])

    def back_near(j, carry):
        out = jnp.dot(band_t[...], d_pad[rows(j * 256, SPAN)], preferred_element_type=F32)
        dn_all[rows(j * 256, 256)] = out.astype(BF16)
        return carry

    def back_far(j, carry):
        out = jnp.dot(band_t[...], d_pad[rows(j * 256, SPAN)], preferred_element_type=F32)
        out += jnp.dot(
            corner_t[rows(j * 256, 256)], d_pad[BAND * BLOCK : TOTAL], preferred_element_type=F32
        )
        dn_all[rows(j * 256, 256)] = out.astype(BF16)
        return carry

    lax.fori_loop(0, far_rows // 2, back_far, 0)
    lax.fori_loop(far_rows // 2, GROUPS, back_near, 0)
    for r in range(SEQ - 1):
        to_seq(S_DN, r, dn_all.at[rows(ahead(r) * TOK, TOK)], dn_back.at[sq]).start()
    dn_back[sq] = dn_all[my_rows]

    for r in range(SEQ - 1):
        from_seq(S_N, r, n_pad.at[rows(PAD + behind(r) * TOK, TOK)])

    g1_buf[...] = jnp.zeros_like(g1_buf)

    def turn(i, carry):
        block = n_pad[rows(PAD + i * 256, 256)]
        wide = block.astype(F32)
        nt_pad[:, lanes(PAD + i * 256, 256)] = block.T
        dn = dn_all[rows(i * 256, 256)].astype(F32)
        g1_buf[...] += jnp.sum((dn * wide).reshape(32, 8, WIDTH), axis=0)
        return carry

    lax.fori_loop(0, GROUPS, turn, 0)
    g1[dp] = g1_buf[...]
    other_dp(lambda r: to_dp(S_G1, r, g1_buf, g1.at[dp]).start())

    def slots(m, carry):
        acc = jnp.zeros((256, 256), F32)
        for i in range(GROUPS):
            acc += jnp.dot(
                d_pad[i * 256 : (i + 1) * 256],
                nt_pad[:, lanes(i * 256 + m * 256, 256)],
                preferred_element_type=F32,
            )
        sums[m] = acc
        return carry

    lax.fori_loop(0, (BAND + 2) // 2, slots, 0)
    for i in range(far_rows):
        for s in range(NSTR):
            col = jnp.broadcast_to(cols[BAND + i : BAND + i + 1, s : s + 1], (BLOCK, WIDTH))
            block = n_pad[PAD : PAD + BLOCK].astype(F32)
            for c in range(1, i + 1):
                other = n_pad[PAD + c * BLOCK : PAD + (c + 1) * BLOCK].astype(F32)
                block = jnp.where(col == c, other, block)
            picked[i, s * BLOCK : (s + 1) * BLOCK] = block.astype(BF16)
    far = jnp.zeros((BLOCK, 2 * BLOCK), F32)
    for i in range(far_rows):
        far += lax.dot_general(
            d_pad[(BAND + i) * BLOCK : (BAND + i + 1) * BLOCK],
            picked[i],
            (((1,), (1,)), ((), ())),
            preferred_element_type=F32,
        )
    for k in range(SLOTS):
        if k < BAND:
            m0, m1 = BAND - 1 - k, BAND - k
            grad_k = (
                sums[m0 // 2, :BLOCK, (m0 % 2) * BLOCK : (m0 % 2 + 1) * BLOCK]
                + sums[m1 // 2, BLOCK:, (m1 % 2) * BLOCK : (m1 % 2 + 1) * BLOCK]
            )
        else:
            grad_k = far[:, (k - BAND) * BLOCK : (k - BAND + 1) * BLOCK]
        if k == 0:
            grad_k = jnp.where(lower, grad_k, 0.0)
        slot_buf[k * BLOCK : (k + 1) * BLOCK] = grad_k.astype(BF16)
    other_dp(
        lambda r: to_dp(
            S_R1, r, slot_buf.at[rows(((dp + r) % DP) * PIECE, PIECE)], r1.at[dp]
        ).start()
    )
    r1[dp] = slot_buf[rows(dp * PIECE, PIECE)]

    bias_t = bias[...].T
    two = 2 * BLOCK
    far_w = jnp.concatenate([weights[BAND], weights[BAND + 1]], axis=1)
    for i in range(GROUPS):
        out = jnp.dot(band[...], n_pad[i * two : i * two + SPAN], preferred_element_type=F32)
        for h in range(2):
            half = out[h * BLOCK : (h + 1) * BLOCK]
            b = 2 * i + h
            if b >= BAND:
                half += jnp.dot(far_w, picked[b - BAND], preferred_element_type=F32)
            half += bias_t[:, b : b + 1]
            mx_all[b * BLOCK : (b + 1) * BLOCK] = half.astype(BF16)

    def send_mixed(r):
        to_seq(S_MX, r, mx_all.at[rows(ahead(r) * TOK, TOK)], mx_back.at[sq]).start()

    other_dp(lambda r: from_dp(S_G1, r, g1.at[(dp + DP - r) % DP]))
    total = jnp.sum(jnp.sum(g1[...], axis=0), axis=0, keepdims=True)
    my_gain = gain[:, lanes(sq * WIDTH, WIDTH)]
    g2[sq] = jnp.broadcast_to(total / (my_gain * math.sqrt(DP * TOTAL)), (8, WIDTH))
    for r in range(SEQ - 1):
        to_seq(S_G2, r, g2.at[sq], g2.at[sq]).start()

    other_dp(lambda r: from_dp(S_R1, r, r1.at[(dp + DP - r) % DP]))

    def sum_piece(t, carry):
        part[t] = jnp.sum(r1[:, rows(t * SUB, SUB), :].astype(F32), axis=0)
        return carry

    lax.fori_loop(0, REDUCERS, sum_piece, 0)
    for r in range(SEQ - 1):
        @pl.when(ahead(r) < REDUCERS)
        def _():
            to_seq(S_R2, r, part.at[ahead(r)], r2.at[sq]).start()

    for r in range(MIX_FIRST):
        send_mixed(r)

    @pl.when(sq < REDUCERS)
    def _():
        r2[sq] = part[sq]
        for r in range(SEQ - 1):
            from_seq(S_R2, r, r2.at[behind(r)])
        r2b[sq] = jnp.sum(r2[...], axis=0)
        for r in range(SEQ - 1):
            to_seq(S_R2B, r, r2b.at[sq], r2b.at[sq]).start()

    for r in range(MIX_FIRST, SEQ - 1):
        send_mixed(r)
    mx_back[sq] = mx_all[my_rows]

    for r in range(SEQ - 1):
        from_seq(S_DN, r, dn_back.at[behind(r)])

    def value_rows(c, carry):
        at = rows(c * CHUNK, CHUNK)
        first = jnp.zeros((CHUNK, WIDTH), F32)
        second = jnp.zeros((CHUNK, WIDTH), F32)
        for p in range(SEQ):
            cut = slice(p * WIDTH, (p + 1) * WIDTH)
            hat_grad = dn_back[p, at].astype(F32) * gain[:, cut]
            first += hat_grad
            second += hat_grad * hat_ref[at, cut]
        mean1 = jnp.sum(first, axis=1, keepdims=True) * (1.0 / FEAT)
        mean2 = jnp.sum(second, axis=1, keepdims=True) * (1.0 / FEAT)
        inv = inv_ref[at][:, :1]
        for p in range(SEQ):
            cut = slice(p * WIDTH, (p + 1) * WIDTH)
            hat_grad = dn_back[p, at].astype(F32) * gain[:, cut]
            out = inv * (hat_grad - mean1 - hat_ref[at, cut] * mean2)
            value_grad[at, cut] = out.astype(BF16)
        return carry

    lax.fori_loop(0, TOK // CHUNK, value_rows, 0)

    for r in range(SEQ - 1):
        @pl.when(behind(r) < REDUCERS)
        def _():
            from_seq(S_R2B, r, r2b.at[behind(r)])

    for t in range(REDUCERS):
        r3_buf[t * SUB : (t + 1) * SUB] = r2b[t].astype(BF16)
    other_dp(lambda r: to_dp(S_R3, r, r3_buf, r3.at[dp]).start())
    r3[dp] = r3_buf[...]

    other_dp(lambda r: from_dp(S_BIAS, r, bias_all.at[(dp + DP - r) % DP]))
    bias_sum = jnp.sum(jnp.sum(bias_all[...], axis=0), axis=0, keepdims=True)
    bias_grad[...] = bias_sum * (1.0 / math.sqrt(DP * FEAT))
    for r in range(SEQ - 1):
        from_seq(S_G2, r, g2.at[behind(r)])
    for p in range(SEQ):
        gain_grad[:, p * WIDTH : (p + 1) * WIDTH] = g2[p, :1]

    def finish(panel):
        at = lanes(panel * WIDTH, WIDTH)
        gated_grad[:, at] = (g_ref[:, at].astype(F32) * mx_back[panel].astype(F32)).astype(BF16)

    finish(sq)
    for r in range(SEQ - 1):
        from_seq(S_MX, r, mx_back.at[behind(r)])
        finish(behind(r))

    scale = 1.0 / math.sqrt(DP * TOTAL * FEAT)
    weight_grad[rows(dp * PIECE, PIECE)] = r3[dp].astype(F32) * scale

    def last(r):
        piece = (dp + DP - r) % DP
        from_dp(S_R3, r, r3.at[piece])
        weight_grad[rows(piece * PIECE, PIECE)] = r3[piece].astype(F32) * scale

    other_dp(last)

    for r in range(SEQ - 1):
        to_seq(S_D, r, d_buf.at[ahead(r)], d_pad.at[my_rows]).wait_send()
        to_seq(S_N, r, n_buf.at[ahead(r)], n_pad.at[my_padded]).wait_send()
        to_seq(S_DN, r, dn_all.at[rows(ahead(r) * TOK, TOK)], dn_back.at[sq]).wait_send()
        to_seq(S_MX, r, mx_all.at[rows(ahead(r) * TOK, TOK)], mx_back.at[sq]).wait_send()
        to_seq(S_G2, r, g2.at[sq], g2.at[sq]).wait_send()

        @pl.when(ahead(r) < REDUCERS)
        def _():
            to_seq(S_R2, r, part.at[ahead(r)], r2.at[sq]).wait_send()

        @pl.when(sq < REDUCERS)
        def _():
            to_seq(S_R2B, r, r2b.at[sq], r2b.at[sq]).wait_send()

    def sent(r):
        to_dp(S_BIAS, r, bias_all.at[dp], bias_all.at[dp]).wait_send()
        to_dp(S_G1, r, g1_buf, g1.at[dp]).wait_send()
        to_dp(
            S_R1, r, slot_buf.at[rows(((dp + r) % DP) * PIECE, PIECE)], r1.at[dp]
        ).wait_send()
        to_dp(S_R3, r, r3_buf, r3.at[dp]).wait_send()

    other_dp(sent)


def shards(gated_part, mixed_part, out_grad, norm_gain, mix_bias, token_mixing_weight, stride_cols):
    vmem = pl.BlockSpec(memory_space=pltpu.VMEM)
    hbm = pl.BlockSpec(memory_space=pl.ANY)
    wide = (TOK, FEAT)
    panels = (SEQ, TOK, WIDTH)
    scratch = [
        (wide, BF16), (wide, BF16), (wide, BF16), (wide, F32), ((TOK, BLOCK), F32),
        (panels, BF16), (panels, BF16),
        ((TOTAL + PAD, WIDTH), BF16), ((TOTAL + PAD, WIDTH), BF16),
        ((WIDTH, TOTAL + SPAN - BLOCK), BF16),
        ((TOTAL, WIDTH), BF16), ((TOTAL, WIDTH), BF16), (panels, BF16), (panels, BF16),
        ((2 * BLOCK, SPAN), BF16), ((2 * BLOCK, SPAN), BF16), ((8 * BLOCK, 8 * BLOCK), BF16),
        ((NSTR, BLOCK, BLOCK), F32), ((8, NSTR * BLOCK, WIDTH), BF16),
        (((BAND + 2) // 2, 256, 256), F32), ((SLOTS * BLOCK, BLOCK), BF16),
        ((DP, PIECE, BLOCK), BF16), ((REDUCERS, SUB, BLOCK), F32), ((SEQ, SUB, BLOCK), F32),
        ((REDUCERS, SUB, BLOCK), F32), ((PIECE, BLOCK), BF16), ((DP, PIECE, BLOCK), BF16),
        ((TOK, BLOCK), F32), ((DP, 8, TOK), F32),
        ((8, WIDTH), F32), ((DP, 8, WIDTH), F32), ((SEQ, 8, WIDTH), F32),
    ]
    outs = pl.pallas_call(
        kernel,
        out_shape=(
            jax.ShapeDtypeStruct(wide, BF16),
            jax.ShapeDtypeStruct(wide, BF16),
            jax.ShapeDtypeStruct((SLOTS * BLOCK, BLOCK), F32),
            jax.ShapeDtypeStruct((1, FEAT), F32),
            jax.ShapeDtypeStruct((1, TOK), F32),
        ),
        in_specs=[hbm, hbm, hbm, vmem, vmem, vmem, vmem],
        out_specs=[vmem] * 5,
        scratch_shapes=[pltpu.VMEM(shape, kind) for shape, kind in scratch]
        + [
            pltpu.SemaphoreType.DMA((3,)),
            pltpu.SemaphoreType.DMA((PHASES, SEQ)),
            pltpu.SemaphoreType.DMA((PHASES, SEQ)),
        ],
        compiler_params=pltpu.CompilerParams(
            collective_id=0, has_side_effects=True, vmem_limit_bytes=56 * 2**20
        ),
    )(
        gated_part[0],
        mixed_part[0],
        out_grad[0],
        norm_gain.reshape(1, FEAT),
        mix_bias.reshape(TOTAL // BLOCK, BLOCK),
        token_mixing_weight,
        stride_cols,
    )
    gated_grad, value_grad, weight_grad, gain_grad, bias_grad = outs
    return (
        gated_grad[None],
        value_grad[None],
        weight_grad.reshape(SLOTS, BLOCK, BLOCK),
        gain_grad.reshape(FEAT),
        bias_grad.reshape(TOK),
    )


def solution(mesh):
    placed = (P("dp", "seq", None), P("dp", "seq", None), P("dp", "seq", None), P(), P(), P(), P())
    return jax.shard_map(
        shards,
        mesh=mesh,
        in_specs=placed,
        out_specs=(P("dp", "seq", None), P("dp", "seq", None), P(), P(), P("seq")),
        check_vma=False,
    )
```

time: 713 us -> 125 us (0.18); the launches traced: 701 us -> 125 us
  waiting for transfers between devices: 288 us -> 0 us
  local copies, waits for them, and re-layouts: 145 us -> 8.21 us
  Pallas kernels: 0 us -> 116 us
  matrix products: 85.8 us -> 0 us
  blocking collectives: 78.9 us -> 0 us
  other arithmetic: 40.2 us -> 0 us
  starting transfers between devices: 32 us -> 0 us
  loops' own time: 16.1 us -> 0 us
  between operations: 14.7 us -> 0.65 us
    psum x1 -> x0, waiting for transfers between devices: 266 us -> none  [shards(): lax.psum((slot_grad, gain_part, bias_part), ('dp', 'seq'))]
    pallas_call x0 -> x1, Pallas kernels: none -> 116 us  [shards(): pl.pallas_call(kernel, out_shape=(jax.ShapeDtypeStruct(wide, BF16), jax.S...]
    dot_general x48 -> x0, matrix products: 85.8 us -> none  [the longest x24 46.4 us: one_group(): return jnp.dot(matrix, piece, preferred_element_type=jnp.float32)]
    psum x1 -> x0, blocking collectives: 78.9 us -> none  [shards(): lax.psum((slot_grad, gain_part, bias_part), ('dp', 'seq'))]
    unnamed x77 -> x14, local copies, waits for them, and re-layouts: 44.2 us -> 8.21 us
    all_to_all x5 -> x0, starting transfers between devices: 32 us -> none  [the longest x1 7.72 us: shards(): lax.all_to_all(to_panels(normed), 'seq', split_axis=1, concat_axis=0, til...]
    slice x2 -> x0, local copies, waits for them, and re-layouts: 24.8 us -> none  [the longest x1 24.7 us: mix_backward(): lax.slice_in_dim(padded, start, start + total_len, axis=0)]
    all_to_all x5 -> x0, waiting for transfers between devices: 21.9 us -> none  [the longest x1 13.7 us: shards(): lax.all_to_all(to_panels(normed), 'seq', split_axis=1, concat_axis=0, til...]
  transfers between devices with their start and end apart: 6 -> 0, of which waited for: 3 -> 0; matrix products, arithmetic and copies ran while one was open for 29% -> 0% of each run, Pallas kernels for 0% -> 0%
where the time goes in v1:
time: 125 us
  Pallas kernels  116 us (93%)
  local copies, waits for them, and re-layouts  8.21 us (7%)
    pallas_call x1, Pallas kernels, shards(): pl.pallas_call(kernel, out_shape=(jax.ShapeDtypeStruct(wide, BF16), jax.S...  116 us
    unnamed x14, local copies, waits for them, and re-layouts  8.21 us

profile of v1, /device:TPU:1, one launch (start us, length us, event | category | flops | bytes accessed | tf_op | source)
XLA Modules:
  0.0 124.6 jit_solution(14436436607408913996)
XLA Ops:
  0.6 1.4 %copy.12.cols = s32[24,2]{1,0:T(8,128)} copy(s32[24,2]{0,1:T(2,128)} %param.13) | data formatting | bytes 384 | tf_op args[6]
  2.0 115.8 %shard_map.110 = (bf16[192,4096]{1,0:T(8,128)(2,1)}, bf16[192,4096]{1,0:T(8,128)(2,1)}, f32[2304,128]{1,0:T(8,128)}, f32[1,4096]{1,0:T(1,128)}, f32[1,192]{1,0:T(1,128)}) custom-call(bf16[192,4096]{1,0:T(8,128)(2,1)} %bitcast.12, bf16[192,4096]{1,0:T(8,128)(2,1)} %bitcast.13, bf16[192,4096]{1,0:T(8,128)(2,1)} %bitcast.14, f32[1,4096]{1,0:T(1,128)} %bitcast.16, ...), custom_call_target="tpu_custom_call" | custom-call | tf_op jit(solution)/shard_map/pallas_call | solution.py:455
  117.8 0.0 copy-start
  117.8 2.8 %copy.18 = bf16[1,192,4096]{2,1,0:T(8,128)(2,1)} copy(bf16[1,192,4096]{2,1,0:T(8,128)(2,1)} %bitcast.11) | data formatting | bytes 3145728
  120.6 0.0 copy-done
  120.6 0.0 copy-start.1
  120.6 1.1 copy.19
  121.7 0.7 copy-done.1
  122.4 0.0 copy-start.2
  122.4 0.0 copy-start.3
  122.4 1.0 copy.20
  123.4 0.0 copy-done.2
  123.4 0.6 copy.21
  124.1 0.0 copy-done.3
  124.1 0.6 copy.22
Async XLA Ops:
  117.8 2.8 %copy-start = (bf16[192,4096]{1,0:T(8,128)(2,1)S(1)}, bf16[192,4096]{1,0:T(8,128)(2,1)}, u32[]{:S(2)}) copy-start(bf16[192,4096]{1,0:T(8,128)(2,1)} %get-tuple-element.11) | copy-start | bytes 4718596
  120.6 1.8 %copy-start.1 = (f32[2304,128]{1,0:T(8,128)S(1)}, f32[2304,128]{1,0:T(8,128)}, u32[]{:S(2)}) copy-start(f32[2304,128]{1,0:T(8,128)} %get-tuple-element.12) | copy-start | bytes 3538948
  122.4 1.0 copy-start.2
  122.4 1.6 %copy-start.3 = (f32[1,192]{1,0:T(1,128)S(1)}, f32[1,192]{1,0:T(1,128)}, u32[]{:S(2)}) copy-start(f32[1,192]{1,0:T(1,128)} %get-tuple-element.14) | copy-start | bytes 2308

commit v2 on v1

--- a/solution.py
+++ b/solution.py
@@ -29,15 +29,28 @@
 GROUPS = TOTAL // (2 * BLOCK)
 SPAN = (BAND + 1) * BLOCK
 PAD = (BAND - 1) * BLOCK
+SUMS = (BAND + 2) * BLOCK
 SLOTS = BAND + NSTR
 PIECE = SLOTS * BLOCK // DP
 SUB = 16
+DEPTH = 8
+HALF = DEPTH * PIECE
 REDUCERS = PIECE // SUB
 CHUNK = 16
 
-S_D, S_N, S_DN, S_MX, S_R1, S_R2, S_R2B, S_R3, S_BIAS, S_G1, S_G2 = range(11)
-PHASES = 11
-MIX_FIRST = 5
+S_D, S_N, S_DN, S_MX, S_R1, S_R2, S_R2B, S_R3, S_BIAS, S_G1, S_G2, S_R0, S_R4 = range(13)
+PHASES = 13
+BACK_FIRST = 6
+MIX_FIRST = 3
+MIX_SECOND = 7
+
+
+def weave(first, second):
+    order = []
+    for i, item in enumerate(first):
+        order.append((True, item))
+        order += [(False, other) for q, other in enumerate(second) if q * len(first) // len(second) == i]
+    return order
 
 
 def rows(start, size):
@@ -49,17 +62,18 @@
 
 
 def kernel(
-    gated, value, grad, gain, bias, weights, cols,
+    gated, value, grad, gain_in, bias_in, weights_in, cols_in,
     gated_grad, value_grad, weight_grad, gain_grad, bias_grad,
-    u_ref, v_ref, g_ref, hat_ref, inv_ref,
-    d_buf, n_buf, d_pad, n_pad, nt_pad, dn_all, mx_all, dn_back, mx_back,
+    u_ref, v_ref, g_ref, gain, bias, weights, cols, hat_ref, inv_ref,
+    d_buf, n_buf, d_pad, n_pad, dn_all, mx_all, dn_back, mx_back,
     band, band_t, corner_t, wt_ref, picked, sums, slot_buf,
-    r1, part, r2, r2b, r3_buf, r3, bias_acc, bias_all, g1_buf, g1, g2,
+    r0, half_buf, r1, part, r2, r2b, r3_buf, r3, bias_acc, bias_all, g1_buf, g1, g2,
     in_sem, ss, rs,
 ):
     dp = lax.axis_index("dp")
     sq = lax.axis_index("seq")
     x, y = sq // 4, sq % 4
+    z, core = dp // 2, dp % 2
 
     def ahead(r):
         dx, dy = OFFSETS[r]
@@ -93,6 +107,24 @@
             device_id=((dp + DP - r) % DP, sq), device_id_type=MESH,
         ).wait_recv()
 
+    def to_z(phase, r, src, dst):
+        return pltpu.make_async_remote_copy(
+            src_ref=src, dst_ref=dst, send_sem=ss.at[phase, r], recv_sem=rs.at[phase, r],
+            device_id=(((z + r) % DEPTH) * 2 + core, sq), device_id_type=MESH,
+        )
+
+    def from_z(phase, r, slot):
+        pltpu.make_async_remote_copy(
+            src_ref=slot, dst_ref=slot, send_sem=ss.at[phase, r], recv_sem=rs.at[phase, r],
+            device_id=(((z + DEPTH - r) % DEPTH) * 2 + core, sq), device_id_type=MESH,
+        ).wait_recv()
+
+    def to_core(phase, src, dst):
+        return pltpu.make_async_remote_copy(
+            src_ref=src, dst_ref=dst, send_sem=ss.at[phase, 0], recv_sem=rs.at[phase, 0],
+            device_id=(z * 2 + 1 - core, sq), device_id_type=MESH,
+        )
+
     def other_dp(body):
         def step(r, carry):
             body(r)
@@ -102,7 +134,12 @@
 
     loads = [
         pltpu.make_async_copy(src, dst, in_sem.at[i])
-        for i, (src, dst) in enumerate(((grad, g_ref), (gated, u_ref), (value, v_ref)))
+        for i, (src, dst) in enumerate(
+            (
+                (grad, g_ref), (gated, u_ref), (value, v_ref), (gain_in, gain),
+                (bias_in, bias), (weights_in, weights), (cols_in, cols),
+            )
+        )
     ]
     for load in loads:
         load.start()
@@ -137,7 +174,8 @@
         to_seq(S_D, r, d_buf.at[panel], d_pad.at[my_rows]).start()
     d_pad[my_rows] = make_d(sq)
 
-    loads[2].wait()
+    for load in loads[2:]:
+        load.wait()
 
     def norm_rows(c, carry):
         at = rows(c * CHUNK, CHUNK)
@@ -198,16 +236,14 @@
         for i in range(far_rows):
             block = jnp.zeros((BLOCK, BLOCK), F32)
             for s in range(NSTR):
-                hit = jnp.broadcast_to(cols[BAND + i : BAND + i + 1, s : s + 1], (BLOCK, BLOCK)) == j
+                hit = jnp.broadcast_to(cols[s : s + 1, BAND + i : BAND + i + 1], (BLOCK, BLOCK)) == j
                 block += jnp.where(hit, wt_ref[s], 0.0)
             corner_t[rows(j * BLOCK, BLOCK), i * BLOCK : (i + 1) * BLOCK] = block.astype(BF16)
         return carry
 
     lax.fori_loop(0, far_rows, corner_row, 0)
-    d_pad[TOTAL:] = jnp.zeros((PAD, WIDTH), BF16)
+    d_pad[TOTAL:] = jnp.zeros((PAD + BLOCK, WIDTH), BF16)
     n_pad[:PAD] = jnp.zeros((PAD, WIDTH), BF16)
-    nt_pad[:, :PAD] = jnp.zeros((WIDTH, PAD), BF16)
-    nt_pad[:, PAD + TOTAL :] = jnp.zeros((WIDTH, BLOCK), BF16)
 
     for r in range(SEQ - 1):
         from_seq(S_D, r, d_pad.at[rows(behind(r) * TOK, TOK)])
@@ -227,8 +263,12 @@
 
     lax.fori_loop(0, far_rows // 2, back_far, 0)
     lax.fori_loop(far_rows // 2, GROUPS, back_near, 0)
-    for r in range(SEQ - 1):
+
+    def send_back(r):
         to_seq(S_DN, r, dn_all.at[rows(ahead(r) * TOK, TOK)], dn_back.at[sq]).start()
+
+    for r in range(BACK_FIRST):
+        send_back(r)
     dn_back[sq] = dn_all[my_rows]
 
     for r in range(SEQ - 1):
@@ -237,9 +277,7 @@
     g1_buf[...] = jnp.zeros_like(g1_buf)
 
     def turn(i, carry):
-        block = n_pad[rows(PAD + i * 256, 256)]
-        wide = block.astype(F32)
-        nt_pad[:, lanes(PAD + i * 256, 256)] = block.T
+        wide = n_pad[rows(PAD + i * 256, 256)].astype(F32)
         dn = dn_all[rows(i * 256, 256)].astype(F32)
         g1_buf[...] += jnp.sum((dn * wide).reshape(32, 8, WIDTH), axis=0)
         return carry
@@ -248,21 +286,21 @@
     g1[dp] = g1_buf[...]
     other_dp(lambda r: to_dp(S_G1, r, g1_buf, g1.at[dp]).start())
 
-    def slots(m, carry):
-        acc = jnp.zeros((256, 256), F32)
-        for i in range(GROUPS):
-            acc += jnp.dot(
-                d_pad[i * 256 : (i + 1) * 256],
-                nt_pad[:, lanes(i * 256 + m * 256, 256)],
-                preferred_element_type=F32,
-            )
-        sums[m] = acc
-        return carry
-
-    lax.fori_loop(0, (BAND + 2) // 2, slots, 0)
+    sums[...] = jnp.zeros_like(sums)
+
+    def slots(j, carry):
+        sums[...] += lax.dot_general(
+            d_pad[rows(j * 256, SUMS)],
+            n_pad[rows(PAD + j * 256, 256)],
+            (((1,), (1,)), ((), ())),
+            preferred_element_type=F32,
+        )
+        return carry
+
+    lax.fori_loop(0, GROUPS, slots, 0)
     for i in range(far_rows):
         for s in range(NSTR):
-            col = jnp.broadcast_to(cols[BAND + i : BAND + i + 1, s : s + 1], (BLOCK, WIDTH))
+            col = jnp.broadcast_to(cols[s : s + 1, BAND + i : BAND + i + 1], (BLOCK, WIDTH))
             block = n_pad[PAD : PAD + BLOCK].astype(F32)
             for c in range(1, i + 1):
                 other = n_pad[PAD + c * BLOCK : PAD + (c + 1) * BLOCK].astype(F32)
@@ -278,22 +316,30 @@
         )
     for k in range(SLOTS):
         if k < BAND:
-            m0, m1 = BAND - 1 - k, BAND - k
             grad_k = (
-                sums[m0 // 2, :BLOCK, (m0 % 2) * BLOCK : (m0 % 2 + 1) * BLOCK]
-                + sums[m1 // 2, BLOCK:, (m1 % 2) * BLOCK : (m1 % 2 + 1) * BLOCK]
+                sums[k * BLOCK : (k + 1) * BLOCK, :BLOCK]
+                + sums[(k + 1) * BLOCK : (k + 2) * BLOCK, BLOCK:]
             )
         else:
             grad_k = far[:, (k - BAND) * BLOCK : (k - BAND + 1) * BLOCK]
         if k == 0:
             grad_k = jnp.where(lower, grad_k, 0.0)
         slot_buf[k * BLOCK : (k + 1) * BLOCK] = grad_k.astype(BF16)
-    other_dp(
-        lambda r: to_dp(
-            S_R1, r, slot_buf.at[rows(((dp + r) % DP) * PIECE, PIECE)], r1.at[dp]
-        ).start()
-    )
-    r1[dp] = slot_buf[rows(dp * PIECE, PIECE)]
+    mine, theirs = rows(core * HALF, HALF), rows((1 - core) * HALF, HALF)
+    swap = to_core(S_R0, slot_buf.at[theirs], r0)
+    swap.start()
+    swap.wait_recv()
+    half_buf[...] = (slot_buf[mine].astype(F32) + r0[...].astype(F32)).astype(BF16)
+
+    def z_rows(r):
+        return rows(((z + r) % DEPTH) * PIECE, PIECE)
+
+    for summed, r in weave(range(1, DEPTH), range(BACK_FIRST, SEQ - 1)):
+        if summed:
+            to_z(S_R1, r, half_buf.at[z_rows(r)], r1.at[z]).start()
+        else:
+            send_back(r)
+    r1[z] = half_buf[z_rows(0)]
 
     bias_t = bias[...].T
     two = 2 * BLOCK
@@ -318,7 +364,8 @@
     for r in range(SEQ - 1):
         to_seq(S_G2, r, g2.at[sq], g2.at[sq]).start()
 
-    other_dp(lambda r: from_dp(S_R1, r, r1.at[(dp + DP - r) % DP]))
+    for r in range(1, DEPTH):
+        from_z(S_R1, r, r1.at[(z + DEPTH - r) % DEPTH])
 
     def sum_piece(t, carry):
         part[t] = jnp.sum(r1[:, rows(t * SUB, SUB), :].astype(F32), axis=0)
@@ -342,9 +389,24 @@
         for r in range(SEQ - 1):
             to_seq(S_R2B, r, r2b.at[sq], r2b.at[sq]).start()
 
-    for r in range(MIX_FIRST, SEQ - 1):
+    for r in range(MIX_FIRST, MIX_SECOND):
         send_mixed(r)
     mx_back[sq] = mx_all[my_rows]
+
+    for r in range(SEQ - 1):
+        @pl.when(behind(r) < REDUCERS)
+        def _():
+            from_seq(S_R2B, r, r2b.at[behind(r)])
+
+    for t in range(REDUCERS):
+        r3_buf[t * SUB : (t + 1) * SUB] = r2b[t].astype(BF16)
+    my_piece = core * DEPTH + z
+    for summed, r in weave(range(1, DEPTH), range(MIX_SECOND, SEQ - 1)):
+        if summed:
+            to_z(S_R3, r, r3_buf, r3.at[my_piece]).start()
+        else:
+            send_mixed(r)
+    r3[my_piece] = r3_buf[...]
 
     for r in range(SEQ - 1):
         from_seq(S_DN, r, dn_back.at[behind(r)])
@@ -370,16 +432,6 @@
 
     lax.fori_loop(0, TOK // CHUNK, value_rows, 0)
 
-    for r in range(SEQ - 1):
-        @pl.when(behind(r) < REDUCERS)
-        def _():
-            from_seq(S_R2B, r, r2b.at[behind(r)])
-
-    for t in range(REDUCERS):
-        r3_buf[t * SUB : (t + 1) * SUB] = r2b[t].astype(BF16)
-    other_dp(lambda r: to_dp(S_R3, r, r3_buf, r3.at[dp]).start())
-    r3[dp] = r3_buf[...]
-
     other_dp(lambda r: from_dp(S_BIAS, r, bias_all.at[(dp + DP - r) % DP]))
     bias_sum = jnp.sum(jnp.sum(bias_all[...], axis=0), axis=0, keepdims=True)
     bias_grad[...] = bias_sum * (1.0 / math.sqrt(DP * FEAT))
@@ -393,19 +445,29 @@
         gated_grad[:, at] = (g_ref[:, at].astype(F32) * mx_back[panel].astype(F32)).astype(BF16)
 
     finish(sq)
-    for r in range(SEQ - 1):
+    for r in range(7):
         from_seq(S_MX, r, mx_back.at[behind(r)])
         finish(behind(r))
 
+    for r in range(1, DEPTH):
+        from_z(S_R3, r, r3.at[core * DEPTH + (z + DEPTH - r) % DEPTH])
+    half = r3.at[pl.ds(core * DEPTH, DEPTH)]
+    pass_on = to_core(S_R4, half, half)
+    pass_on.start()
     scale = 1.0 / math.sqrt(DP * TOTAL * FEAT)
-    weight_grad[rows(dp * PIECE, PIECE)] = r3[dp].astype(F32) * scale
-
-    def last(r):
-        piece = (dp + DP - r) % DP
-        from_dp(S_R3, r, r3.at[piece])
-        weight_grad[rows(piece * PIECE, PIECE)] = r3[piece].astype(F32) * scale
-
-    other_dp(last)
+
+    def scale_half(which):
+        for t in range(DEPTH):
+            piece = which * DEPTH + t
+            weight_grad[rows(piece * PIECE, PIECE)] = r3[piece].astype(F32) * scale
+
+    scale_half(core)
+    for r in range(7, SEQ - 1):
+        from_seq(S_MX, r, mx_back.at[behind(r)])
+        finish(behind(r))
+    other = r3.at[pl.ds((1 - core) * DEPTH, DEPTH)]
+    to_core(S_R4, other, other).wait_recv()
+    scale_half(1 - core)
 
     for r in range(SEQ - 1):
         to_seq(S_D, r, d_buf.at[ahead(r)], d_pad.at[my_rows]).wait_send()
@@ -425,29 +487,30 @@
     def sent(r):
         to_dp(S_BIAS, r, bias_all.at[dp], bias_all.at[dp]).wait_send()
         to_dp(S_G1, r, g1_buf, g1.at[dp]).wait_send()
-        to_dp(
-            S_R1, r, slot_buf.at[rows(((dp + r) % DP) * PIECE, PIECE)], r1.at[dp]
-        ).wait_send()
-        to_dp(S_R3, r, r3_buf, r3.at[dp]).wait_send()
-
     other_dp(sent)
+    swap.wait_send()
+    pass_on.wait_send()
+    for r in range(1, DEPTH):
+        to_z(S_R1, r, half_buf.at[z_rows(r)], r1.at[z]).wait_send()
+        to_z(S_R3, r, r3_buf, r3.at[my_piece]).wait_send()
 
 
 def shards(gated_part, mixed_part, out_grad, norm_gain, mix_bias, token_mixing_weight, stride_cols):
     vmem = pl.BlockSpec(memory_space=pltpu.VMEM)
-    hbm = pl.BlockSpec(memory_space=pl.ANY)
+    hbm = pl.BlockSpec(memory_space=pltpu.HBM)
     wide = (TOK, FEAT)
     panels = (SEQ, TOK, WIDTH)
     scratch = [
-        (wide, BF16), (wide, BF16), (wide, BF16), (wide, F32), ((TOK, BLOCK), F32),
+        (wide, BF16), (wide, BF16), (wide, BF16), ((1, FEAT), F32), ((TOTAL // BLOCK, BLOCK), F32),
+        ((SLOTS, BLOCK, BLOCK), BF16), ((NSTR, TOTAL // BLOCK), jnp.int32), (wide, F32), ((TOK, BLOCK), F32),
         (panels, BF16), (panels, BF16),
-        ((TOTAL + PAD, WIDTH), BF16), ((TOTAL + PAD, WIDTH), BF16),
-        ((WIDTH, TOTAL + SPAN - BLOCK), BF16),
+        ((TOTAL + PAD + BLOCK, WIDTH), BF16), ((TOTAL + PAD, WIDTH), BF16),
         ((TOTAL, WIDTH), BF16), ((TOTAL, WIDTH), BF16), (panels, BF16), (panels, BF16),
         ((2 * BLOCK, SPAN), BF16), ((2 * BLOCK, SPAN), BF16), ((8 * BLOCK, 8 * BLOCK), BF16),
         ((NSTR, BLOCK, BLOCK), F32), ((8, NSTR * BLOCK, WIDTH), BF16),
-        (((BAND + 2) // 2, 256, 256), F32), ((SLOTS * BLOCK, BLOCK), BF16),
-        ((DP, PIECE, BLOCK), BF16), ((REDUCERS, SUB, BLOCK), F32), ((SEQ, SUB, BLOCK), F32),
+        ((SUMS, 256), F32), ((SLOTS * BLOCK, BLOCK), BF16),
+        ((HALF, BLOCK), BF16), ((HALF, BLOCK), BF16),
+        ((DEPTH, PIECE, BLOCK), BF16), ((REDUCERS, SUB, BLOCK), F32), ((SEQ, SUB, BLOCK), F32),
         ((REDUCERS, SUB, BLOCK), F32), ((PIECE, BLOCK), BF16), ((DP, PIECE, BLOCK), BF16),
         ((TOK, BLOCK), F32), ((DP, 8, TOK), F32),
         ((8, WIDTH), F32), ((DP, 8, WIDTH), F32), ((SEQ, 8, WIDTH), F32),
@@ -461,11 +524,11 @@
             jax.ShapeDtypeStruct((1, FEAT), F32),
             jax.ShapeDtypeStruct((1, TOK), F32),
         ),
-        in_specs=[hbm, hbm, hbm, vmem, vmem, vmem, vmem],
+        in_specs=[hbm] * 7,
         out_specs=[vmem] * 5,
         scratch_shapes=[pltpu.VMEM(shape, kind) for shape, kind in scratch]
         + [
-            pltpu.SemaphoreType.DMA((3,)),
+            pltpu.SemaphoreType.DMA((7,)),
             pltpu.SemaphoreType.DMA((PHASES, SEQ)),
             pltpu.SemaphoreType.DMA((PHASES, SEQ)),
         ],
@@ -479,7 +542,7 @@
         norm_gain.reshape(1, FEAT),
         mix_bias.reshape(TOTAL // BLOCK, BLOCK),
         token_mixing_weight,
-        stride_cols,
+        stride_cols.T,
     )
     gated_grad, value_grad, weight_grad, gain_grad, bias_grad = outs
     return (

time: 125 us -> 115 us (0.920)
  Pallas kernels: 116 us -> 106 us
  local copies, waits for them, and re-layouts: 8.21 us -> 6.85 us
    pallas_call x1, Pallas kernels: 116 us -> 106 us  [shards(): pl.pallas_call(kernel, out_shape=(jax.ShapeDtypeStruct(wide, BF16), jax.S...]
    unnamed x14 -> x13, local copies, waits for them, and re-layouts: 8.21 us -> 6.85 us
where the time goes in v2:
time: 115 us; the launch traced here: 114 us
  Pallas kernels  106 us (92%)
  local copies, waits for them, and re-layouts  6.85 us (6%)
    pallas_call x1, Pallas kernels, shards(): pl.pallas_call(kernel, out_shape=(jax.ShapeDtypeStruct(wide, BF16), jax.S...  106 us
    unnamed x13, local copies, waits for them, and re-layouts  6.85 us

profile of v2, /device:TPU:1, one launch (start us, length us, event | category | flops | bytes accessed | tf_op | source)
XLA Modules:
  0.0 113.6 jit_solution(13985939018270254770)
XLA Ops:
  0.6 106.1 %shard_map.110 = (bf16[192,4096]{1,0:T(8,128)(2,1)}, bf16[192,4096]{1,0:T(8,128)(2,1)}, f32[2304,128]{1,0:T(8,128)}, f32[1,4096]{1,0:T(1,128)}, f32[1,192]{1,0:T(1,128)}) custom-call(bf16[192,4096]{1,0:T(8,128)(2,1)} %bitcast.13, bf16[192,4096]{1,0:T(8,128)(2,1)} %bitcast.14, bf16[192,4096]{1,0:T(8,128)(2,1)} %bitcast.15, f32[1,4096]{1,0:T(1,128)} %bitcast.17, ...), custom_call_target="tpu_custom_call" | custom-call | tf_op jit(solution)/shard_map/pallas_call | solution.py:518
  106.7 0.0 copy-start
  106.7 2.8 %copy.17 = bf16[1,192,4096]{2,1,0:T(8,128)(2,1)} copy(bf16[1,192,4096]{2,1,0:T(8,128)(2,1)} %bitcast.12) | data formatting | bytes 3145728
  109.5 0.0 copy-done
  109.5 0.0 copy-start.1
  109.5 1.1 %copy.18 = bf16[1,192,4096]{2,1,0:T(8,128)(2,1)} copy(bf16[1,192,4096]{2,1,0:T(8,128)(2,1)S(1)} %bitcast.11) | data formatting | bytes 3145728
  110.7 0.7 copy-done.1
  111.4 0.0 copy-start.2
  111.4 0.0 copy-start.3
  111.4 1.0 copy.19
  112.4 0.0 copy-done.2
  112.4 0.6 copy.20
  113.0 0.0 copy-done.3
  113.0 0.6 copy.21
Async XLA Ops:
  106.7 2.8 %copy-start = (bf16[192,4096]{1,0:T(8,128)(2,1)S(1)}, bf16[192,4096]{1,0:T(8,128)(2,1)}, u32[]{:S(2)}) copy-start(bf16[192,4096]{1,0:T(8,128)(2,1)} %get-tuple-element.11) | copy-start | bytes 4718596
  109.5 1.8 %copy-start.1 = (f32[2304,128]{1,0:T(8,128)S(1)}, f32[2304,128]{1,0:T(8,128)}, u32[]{:S(2)}) copy-start(f32[2304,128]{1,0:T(8,128)} %get-tuple-element.12) | copy-start | bytes 3538948
  111.4 1.0 copy-start.2
  111.4 1.6 %copy-start.3 = (f32[1,192]{1,0:T(1,128)S(1)}, f32[1,192]{1,0:T(1,128)}, u32[]{:S(2)}) copy-start(f32[1,192]{1,0:T(1,128)} %get-tuple-element.14) | copy-start | bytes 2308

commit v3 on v2

--- a/solution.py
+++ b/solution.py
@@ -40,9 +40,9 @@
 
 S_D, S_N, S_DN, S_MX, S_R1, S_R2, S_R2B, S_R3, S_BIAS, S_G1, S_G2, S_R0, S_R4 = range(13)
 PHASES = 13
-BACK_FIRST = 6
-MIX_FIRST = 3
-MIX_SECOND = 7
+BACK_FIRST = 9
+MIX_FIRST = 1
+MIX_SECOND = 4
 
 
 def weave(first, second):

time: 115 us -> 110 us (0.957); the launches traced: 114 us -> 110 us
  Pallas kernels: 106 us -> 102 us
    pallas_call x1, Pallas kernels: 106 us -> 102 us  [shards(): pl.pallas_call(kernel, out_shape=(jax.ShapeDtypeStruct(wide, BF16), jax.S...]
where the time goes in v3:
time: 110 us
  Pallas kernels  102 us (93%)
  local copies, waits for them, and re-layouts  6.85 us (6%)
    pallas_call x1, Pallas kernels, shards(): pl.pallas_call(kernel, out_shape=(jax.ShapeDtypeStruct(wide, BF16), jax.S...  102 us
    unnamed x13, local copies, waits for them, and re-layouts  6.85 us

profile of v3, /device:TPU:1, one launch (start us, length us, event | category | flops | bytes accessed | tf_op | source)
XLA Modules:
  0.0 109.9 jit_solution(3745783667309932362)
XLA Ops:
  0.6 102.4 %shard_map.110 = (bf16[192,4096]{1,0:T(8,128)(2,1)}, bf16[192,4096]{1,0:T(8,128)(2,1)}, f32[2304,128]{1,0:T(8,128)}, f32[1,4096]{1,0:T(1,128)}, f32[1,192]{1,0:T(1,128)}) custom-call(bf16[192,4096]{1,0:T(8,128)(2,1)} %bitcast.13, bf16[192,4096]{1,0:T(8,128)(2,1)} %bitcast.14, bf16[192,4096]{1,0:T(8,128)(2,1)} %bitcast.15, f32[1,4096]{1,0:T(1,128)} %bitcast.17, ...), custom_call_target="tpu_custom_call" | custom-call | tf_op jit(solution)/shard_map/pallas_call | solution.py:518
  103.0 0.0 copy-start
  103.0 2.8 %copy.17 = bf16[1,192,4096]{2,1,0:T(8,128)(2,1)} copy(bf16[1,192,4096]{2,1,0:T(8,128)(2,1)} %bitcast.12) | data formatting | bytes 3145728
  105.8 0.0 copy-done
  105.8 0.0 copy-start.1
  105.8 1.1 %copy.18 = bf16[1,192,4096]{2,1,0:T(8,128)(2,1)} copy(bf16[1,192,4096]{2,1,0:T(8,128)(2,1)S(1)} %bitcast.11) | data formatting | bytes 3145728
  107.0 0.7 copy-done.1
  107.7 0.0 copy-start.2
  107.7 0.0 copy-start.3
  107.7 1.0 copy.19
  108.7 0.0 copy-done.2
  108.7 0.6 copy.20
  109.3 0.0 copy-done.3
  109.3 0.6 copy.21
Async XLA Ops:
  103.0 2.8 %copy-start = (bf16[192,4096]{1,0:T(8,128)(2,1)S(1)}, bf16[192,4096]{1,0:T(8,128)(2,1)}, u32[]{:S(2)}) copy-start(bf16[192,4096]{1,0:T(8,128)(2,1)} %get-tuple-element.11) | copy-start | bytes 4718596
  105.8 1.8 %copy-start.1 = (f32[2304,128]{1,0:T(8,128)S(1)}, f32[2304,128]{1,0:T(8,128)}, u32[]{:S(2)}) copy-start(f32[2304,128]{1,0:T(8,128)} %get-tuple-element.12) | copy-start | bytes 3538948
  107.7 1.0 copy-start.2
  107.7 1.6 %copy-start.3 = (f32[1,192]{1,0:T(1,128)S(1)}, f32[1,192]{1,0:T(1,128)}, u32[]{:S(2)}) copy-start(f32[1,192]{1,0:T(1,128)} %get-tuple-element.14) | copy-start | bytes 2308

commit v4 on v3

--- a/solution.py
+++ b/solution.py
@@ -41,8 +41,8 @@
 S_D, S_N, S_DN, S_MX, S_R1, S_R2, S_R2B, S_R3, S_BIAS, S_G1, S_G2, S_R0, S_R4 = range(13)
 PHASES = 13
 BACK_FIRST = 9
-MIX_FIRST = 1
-MIX_SECOND = 4
+MIX_FIRST = 0
+MIX_SECOND = 2
 
 
 def weave(first, second):

time: 110 us -> 112 us (1.018); the launches traced: 110 us -> 110 us
  no operation moved by 1% of the time
where the time goes in v4:
time: 112 us; the launch traced here: 110 us
  Pallas kernels  103 us (92%)
  local copies, waits for them, and re-layouts  6.85 us (6%)
    pallas_call x1, Pallas kernels, shards(): pl.pallas_call(kernel, out_shape=(jax.ShapeDtypeStruct(wide, BF16), jax.S...  103 us
    unnamed x13, local copies, waits for them, and re-layouts  6.85 us

profile of v4, /device:TPU:1, one launch (start us, length us, event | category | flops | bytes accessed | tf_op | source)
XLA Modules:
  0.0 110.4 jit_solution(17387850528067821303)
XLA Ops:
  0.6 102.9 %shard_map.110 = (bf16[192,4096]{1,0:T(8,128)(2,1)}, bf16[192,4096]{1,0:T(8,128)(2,1)}, f32[2304,128]{1,0:T(8,128)}, f32[1,4096]{1,0:T(1,128)}, f32[1,192]{1,0:T(1,128)}) custom-call(bf16[192,4096]{1,0:T(8,128)(2,1)} %bitcast.13, bf16[192,4096]{1,0:T(8,128)(2,1)} %bitcast.14, bf16[192,4096]{1,0:T(8,128)(2,1)} %bitcast.15, f32[1,4096]{1,0:T(1,128)} %bitcast.17, ...), custom_call_target="tpu_custom_call" | custom-call | tf_op jit(solution)/shard_map/pallas_call | solution.py:518
  103.6 0.0 copy-start
  103.6 2.8 %copy.17 = bf16[1,192,4096]{2,1,0:T(8,128)(2,1)} copy(bf16[1,192,4096]{2,1,0:T(8,128)(2,1)} %bitcast.12) | data formatting | bytes 3145728
  106.4 0.0 copy-done
  106.4 0.0 copy-start.1
  106.4 1.1 %copy.18 = bf16[1,192,4096]{2,1,0:T(8,128)(2,1)} copy(bf16[1,192,4096]{2,1,0:T(8,128)(2,1)S(1)} %bitcast.11) | data formatting | bytes 3145728
  107.5 0.7 copy-done.1
  108.2 0.0 copy-start.2
  108.2 0.0 copy-start.3
  108.2 1.0 copy.19
  109.3 0.0 copy-done.2
  109.3 0.6 copy.20
  109.9 0.0 copy-done.3
  109.9 0.6 copy.21
Async XLA Ops:
  103.6 2.8 %copy-start = (bf16[192,4096]{1,0:T(8,128)(2,1)S(1)}, bf16[192,4096]{1,0:T(8,128)(2,1)}, u32[]{:S(2)}) copy-start(bf16[192,4096]{1,0:T(8,128)(2,1)} %get-tuple-element.11) | copy-start | bytes 4718596
  106.4 1.8 %copy-start.1 = (f32[2304,128]{1,0:T(8,128)S(1)}, f32[2304,128]{1,0:T(8,128)}, u32[]{:S(2)}) copy-start(f32[2304,128]{1,0:T(8,128)} %get-tuple-element.12) | copy-start | bytes 3538948
  108.2 1.0 copy-start.2
  108.2 1.6 %copy-start.3 = (f32[1,192]{1,0:T(1,128)S(1)}, f32[1,192]{1,0:T(1,128)}, u32[]{:S(2)}) copy-start(f32[1,192]{1,0:T(1,128)} %get-tuple-element.14) | copy-start | bytes 2308
